TPU v7x, 512 devices: a whole 4x8x8 slice. The times are simulated.
512 devices in a mesh: row: 16 (over x, z_hi), col: 32 (over z_lo, y, core).
Axes of the slice: x: 4, y: 8, z: 8 (z_hi: 4, z_lo: 2; z = z_hi * 2 + z_lo), core: 2. Of those that a mesh axis runs over, the one named last changes fastest.
Arguments:
- activations: bfloat16 [16384, 768], P('row', 'col'), may hold values from -6 to 6
- partner: int32 [64], replicated, may hold values from 0 to 63, each once
- mix_weight: int32 [64], replicated, may hold values from 0 to 256
- weight: bfloat16 [768, 24576], P(None, 'col'), may hold values from -0.15625 to 0.15625
- bias: float32 [24576], P('col'), may hold values from -3 to 3
- earlier: bfloat16 [16384, 24576], P('row', 'col'), may hold values from -5 to 5
- cotangent: bfloat16 [16384, 24576], P('row', 'col'), may hold values from -6 to 6
Outputs:
- hidden: bfloat16 [16384, 24576], P('row', 'col')
- weight_grad: float32 [768, 24576], P('row', 'col')
Inputs may be any that keep to these rules, and one draw needn't show every extreme that they name: `partner`: each image is named exactly once.
All inputs are finite; a program needn't handle non-finite values.
Results may differ from a plain program's by a relative error of at most 0.015.
Values may be sent and summed in bfloat16 or wider, within the bound.
A program may use at most 64 MiB of HBM per device.

v0:
```python
import jax
import jax.numpy as jnp
from jax import lax
from jax.sharding import PartitionSpec as P

PATCHES = 256
IMG_DEV = 4


def slope(preact):
    normal_cdf = 0.5 * (1.0 + lax.erf(preact * 0.7071067811865476))
    density = jnp.exp(-0.5 * preact * preact) * 0.3989422804014327
    return normal_cdf + preact * density


def local(activations, partner, mix_weight, weight, bias, earlier, cotangent):
    width = activations.shape[1]
    every_image = lax.all_gather(activations, "row", axis=0, tiled=True)
    image_count = every_image.shape[0] // PATCHES
    first_image = lax.axis_index("row") * IMG_DEV
    my_partner = lax.dynamic_slice_in_dim(partner, first_image, IMG_DEV)
    my_mix = lax.dynamic_slice_in_dim(mix_weight, first_image, IMG_DEV)
    other = every_image.reshape(image_count, PATCHES, width)[my_partner]
    share = (my_mix.astype(jnp.float32) / 256.0)[:, None, None]
    own_images = activations.reshape(IMG_DEV, PATCHES, width).astype(jnp.float32)
    blended = (share * own_images + (1.0 - share) * other.astype(jnp.float32)).astype(jnp.bfloat16)
    blended = blended.reshape(activations.shape[0], width)
    gathered = lax.all_gather(blended, "col", axis=1, tiled=True)
    product = jnp.dot(gathered, weight, preferred_element_type=jnp.float32)
    preact = earlier.astype(jnp.float32) + product + bias[None, :]
    normal_cdf = 0.5 * (1.0 + lax.erf(preact * 0.7071067811865476))
    hidden = (preact * normal_cdf).astype(jnp.bfloat16)
    grad_pre = (cotangent.astype(jnp.float32) * slope(preact)).astype(jnp.bfloat16)
    weight_grad = lax.psum_scatter(
        lax.dot_general(
            gathered, grad_pre, (((0,), (0,)), ((), ())), preferred_element_type=jnp.float32
        ).astype(jnp.bfloat16),
        "row",
        scatter_dimension=0,
        tiled=True,
    ).astype(jnp.float32)
    return (hidden, weight_grad)


def solution(mesh):
    return jax.shard_map(
        local,
        mesh=mesh,
        in_specs=(
            P("row", "col"),
            P(),
            P(),
            P(None, "col"),
            P("col"),
            P("row", "col"),
            P("row", "col"),
        ),
        out_specs=(P("row", "col"), P("row", "col")),
        check_vma=False,
    )
```

profile of v0, /device:TPU:1, one launch (start us, length us, event | category | flops | bytes accessed | tf_op | source)
XLA Modules:
  0.0 234.6 jit_solution(4898058432803832477)
XLA Ops:
  7.2 0.0 copy-start
  7.2 0.0 copy-start.1
  7.2 0.0 copy-start.2
  7.2 0.0 copy-start.5
  7.2 0.0 all-gather.2.cloned.1.call-start
  7.3 48.1 %all_gather.6 = bf16[16384,24]{0,1:T(8,128)(2,1)S(1)} all-gather(bf16[1024,24]{0,1:T(8,128)(2,1)} %param.7), channel_id=1, replica_groups=mesh['row'=16,'col'=32] {'row'}, dimensions={0}, use_global_device_ids=true | all-gather | bytes 835584 | tf_op jit(solution)/shard_map/all_gather | solution.py:18
  55.3 0.1 copy.16
  55.4 0.7 compare_select_fusion
  56.1 0.5 gather_fusion
  56.7 0.0 copy-done.2
  56.7 0.1 broadcast_subtract_fusion
  56.8 0.1 broadcast_bitcast_fusion
  56.9 0.0 copy-done.1
  56.9 0.6 add_convert_fusion
  57.5 0.0 all-gather.2.cloned.1.call-update
  57.6 0.0 copy-start.3
  57.6 0.0 reduce-scatter.2.cloned.1.call-start
  57.6 69.7 %all-gather.2.cloned.1.call-done = bf16[1024,768]{0,1:T(8,128)(2,1)} async-done(((bf16[1024,24]{0,1:T(8,128)(2,1)}), bf16[1024,768]{0,1:T(8,128)(2,1)}) %all-gather.2.cloned.1.call-update) | async-done | bytes 1572880 | tf_op jit(solution)/shard_map/all_gather | solution.py:28
  127.3 0.0 copy-done
  127.3 0.0 copy-done.5
  127.3 0.0 copy-start.4
  127.3 5.2 %multiply_convert_fusion = (bf16[1024,768]{1,0:T(8,128)(2,1)}, f32[1024,768]{1,0:T(8,128)S(1)}) fusion(f32[768]{0:T(1024)S(1)} %copy-done.5, bf16[1024,768]{0,1:T(8,128)(2,1)} %all-gather.2.cloned.1.call-done, bf16[768,768]{1,0:T(8,128)(2,1)S(1)} %copy-done, bf16[1024,768]{1,0:T(8,128)(2,1)} %param.12), kind=kOutput, calls=%fused_computation.8 | convolution fusion | flops 1214251008 | bytes 9047040 | tf_op jit(solution)/shard_map/dot_general | solution.py:29
  132.5 0.0 copy-done.3
  132.5 0.0 copy-done.4
  132.5 3.2 %fusion.10 = bf16[768,768]{1,0:T(8,128)(2,1)} fusion(bf16[1024,768]{0,1:T(8,128)(2,1)S(1)} %copy-done.4, f32[1024,768]{1,0:T(8,128)S(1)} %get-tuple-element.5, bf16[1024,768]{1,0:T(8,128)(2,1)S(1)} %copy-done.3), kind=kOutput, calls=%fused_computation.14 | convolution fusion | flops 1217200128 | bytes 7471104 | tf_op jit(solution)/shard_map/dot_general | solution.py:35
  135.7 0.0 reduce-scatter.2.cloned.1.call-update
  135.7 90.5 %reduce-scatter.2.cloned.1.call-done = bf16[48,768]{1,0:T(8,128)(2,1)} async-done(((bf16[768,768]{1,0:T(8,128)(2,1)}), bf16[48,768]{1,0:T(8,128)(2,1)}) %reduce-scatter.2.cloned.1.call-update) | async-done | bytes 73744 | tf_op jit(solution)/shard_map/reduce_scatter | solution.py:34
  226.2 1.6 convert_element_type.46
  (5 shorter events, 0.0 us)
Async XLA Ops:
  7.2 120.1 %copy-start = (bf16[768,768]{1,0:T(8,128)(2,1)S(1)}, bf16[768,768]{1,0:T(8,128)(2,1)}, u32[]{:S(2)}) copy-start(bf16[768,768]{1,0:T(8,128)(2,1)} %param.10) | copy-start | bytes 3538948
  7.2 49.7 %copy-start.1 = (bf16[1024,24]{0,1:T(8,128)(2,1)S(1)}, bf16[1024,24]{0,1:T(8,128)(2,1)}, u32[]{:S(2)}) copy-start(bf16[1024,24]{0,1:T(8,128)(2,1)} %param.7) | copy-start | bytes 147460
  7.2 49.5 %copy-start.2 = (s32[64]{0:T(128)S(1)}, s32[64]{0:T(128)}, u32[]{:S(2)}) copy-start(s32[64]{0:T(128)} %param.9) | copy-start | bytes 772
  7.2 120.1 %copy-start.5 = (f32[768]{0:T(1024)S(1)}, f32[768]{0:T(1024)}, u32[]{:S(2)}) copy-start(f32[768]{0:T(1024)} %param.11) | copy-start | bytes 9220
  7.2 120.1 %all-gather.2.cloned.1.call-start = ((), (), s32[]{:S(2)}) async-start(), calls=%async_computation.1 | async-start | bytes 1622016 | tf_op jit(solution)/shard_map/all_gather | solution.py:28
  57.6 75.0 %copy-start.3 = (bf16[1024,768]{1,0:T(8,128)(2,1)S(1)}, bf16[1024,768]{1,0:T(8,128)(2,1)}, u32[]{:S(2)}) copy-start(bf16[1024,768]{1,0:T(8,128)(2,1)} %param.13) | copy-start | bytes 4718596
  57.6 168.6 %reduce-scatter.2.cloned.1.call-start = ((), (), s32[]{:S(2)}) async-start(), calls=%async_computation.2 | async-start | bytes 1253376 | tf_op jit(solution)/shard_map/reduce_scatter | solution.py:34
  127.3 5.2 %copy-start.4 = (bf16[1024,768]{0,1:T(8,128)(2,1)S(1)}, bf16[1024,768]{0,1:T(8,128)(2,1)}, u32[]{:S(2)}) copy-start(bf16[1024,768]{0,1:T(8,128)(2,1)} %all-gather.2.cloned.1.call-done) | copy-start | bytes 4718596
Sparse Core Ops, SparseCore 0:
  57.7 69.5 all-gather.1
  135.8 90.2 reduce-scatter.1
where the time goes:
time: 236 us; the launch traced here: 235 us
  waiting for transfers between devices  160 us (68%)
  blocking collectives  48.1 us (20%)
  between operations  14.1 us (6%)
  matrix products  8.38 us (4%)
  other arithmetic  3.03 us (1%)
    reduce_scatter x1, waiting for transfers between devices, local(): lax.psum_scatter(lax.dot_general(gathered, grad_pre, (((0,), (0,)), ((),...  90.5 us
    all_gather x1, waiting for transfers between devices, local(): gathered = lax.all_gather(blended, 'col', axis=1, tiled=True)  69.7 us
    all_gather x1, blocking collectives, local(): every_image = lax.all_gather(activations, 'row', axis=0, tiled=True)  48.1 us
    dot_general x1, matrix products, local(): product = jnp.dot(gathered, weight, preferred_element_type=jnp.float32)  5.21 us
  transfers between devices with their start and end apart: 2, of which 2 were waited for; matrix products, arithmetic and copies ran while one was open for 0% of the time, Pallas kernels for 0%

commit v1 on v0

v1 whole, which is shorter than its diff:
```python
import jax
import jax.numpy as jnp
from jax import lax
from jax.experimental import pallas as pl
from jax.experimental.pallas import tpu as pltpu
from jax.sharding import PartitionSpec as P

X, Z_HI, Z_LO, Y = 4, 4, 2, 8
CHIPS = Z_LO * Y
PATCHES = 256
HALF = 512
TOK = 1024
K_DEV, K_CHIP, K_ALL = 24, 48, 768
FF_DEV, FB = 768, 256
NF = FF_DEV // FB
X_ROWS, OUT_ROWS = K_ALL // X, K_ALL // (X * Z_HI)
TILE = 256
HOPS = Y // 2


def kernel(
    partner, mix, act, weight_in, bias, earlier_in, cot_in,
    hidden_out, grad_out,
    ax, images, own, sel, cand, ball, blend_t, weight, earlier, cot, hidden, grad, term, rx, zs, rz,
    send_a, recv_a, send_p, recv_p, send_z, recv_z, send_y, recv_y, send_s, recv_s,
    send_rx, recv_rx, send_rz, recv_rz, local_a, local_in, local_out,
):
    row, col = lax.axis_index("row"), lax.axis_index("col")
    x, zh = lax.div(row, Z_HI), lax.rem(row, Z_HI)
    chip, core = lax.div(col, 2), lax.rem(col, 2)
    zl, y = lax.div(chip, Y), lax.rem(chip, Y)
    other_core = 1 - core
    f32, bf16 = jnp.float32, jnp.bfloat16

    def device(dx=0, dz=0, dl=0, dy=0, dh=0):
        r = lax.rem(x + dx, X) * Z_HI + lax.rem(zh + dz, Z_HI)
        c = (lax.rem(zl + dl, Z_LO) * Y + lax.rem(y + dy, Y)) * 2 + lax.rem(core + dh, 2)
        return {"row": r, "col": c}

    def remote(src, dst, send, recv, to):
        return pltpu.make_async_remote_copy(
            src_ref=src, dst_ref=dst, send_sem=send, recv_sem=recv,
            device_id=to, device_id_type=pl.DeviceIdType.MESH,
        )

    loads = [
        pltpu.make_async_copy(weight_in, weight, local_in.at[0]),
        pltpu.make_async_copy(earlier_in, earlier, local_in.at[1]),
        pltpu.make_async_copy(cot_in, cot, local_in.at[2]),
    ]
    mine = [
        pltpu.make_async_copy(act, ax.at[x], local_a.at[0]),
        pltpu.make_async_copy(act.at[:, pl.ds(pl.multiple_of(core * HALF, HALF), HALF)], own.at[0], local_a.at[1]),
    ]
    for copy in mine:
        copy.start()

    barrier = pltpu.get_barrier_semaphore()
    peers = [device(dx=d) for d in range(1, X)]
    peers += [device(dz=d, dh=h) for d in range(Z_HI) for h in range(2) if d or h]
    peers += [device(dl=1), device(dy=1), device(dy=Y - 1)]
    for peer in peers:
        pl.semaphore_signal(barrier, inc=1, device_id=peer, device_id_type=pl.DeviceIdType.MESH)
    pl.semaphore_wait(barrier, len(peers))

    first = [remote(act, ax.at[x], send_a.at[d], recv_a.at[d], device(dx=d)) for d in (2, 1, 3)]
    first.append(
        remote(
            act.at[:, pl.ds(pl.multiple_of(other_core * HALF, HALF), HALF)],
            own.at[1], send_a.at[0], recv_a.at[0], device(dh=1),
        )
    )
    for copy in first:
        copy.start()
    for copy in loads:
        copy.start()
    mine[0].wait()
    for copy in first[:3]:
        copy.wait_recv()
    for i in range(X):
        for j in range(4):
            images[i * 4 + j] = ax[i, :, j * PATCHES : (j + 1) * PATCHES]

    second = []
    for d, h in ((2, 0), (2, 1), (1, 0), (1, 1), (3, 0), (3, 1), (0, 1), (0, 0)):
        to_row = x * Z_HI + lax.rem(zh + d, Z_HI)
        to_core = lax.rem(core + h, 2)
        for i in range(2):
            image = partner[to_row * 4 + to_core * 2 + i]
            value = images[lax.div(image, 16) * 4 + lax.rem(image, 4)]
            span = slice(i * PATCHES, (i + 1) * PATCHES)
            if d or h:
                sel[d, h, :, span] = value
            else:
                cand[0, 0, :, span] = value
        if d or h:
            copy = remote(sel.at[d, h], cand.at[d, h], send_p.at[d, h], recv_p.at[d, h], device(dz=d, dh=h))
            copy.start()
            second.append(copy)
    mine[1].wait()
    first[3].wait_recv()
    for copy in second:
        copy.wait_recv()

    for i in range(2):
        image = row * 4 + core * 2 + i
        source = lax.rem(lax.div(partner[image], 4), Z_HI)
        slot = lax.rem(zh - source + Z_HI, Z_HI)
        share = mix[image].astype(f32) / 256.0
        span = slice(i * PATCHES, (i + 1) * PATCHES)
        parts = []
        for k in range(2):
            rel = lax.rem(core + k, 2)
            parts.append(share * own[rel, :, span].astype(f32) + (1.0 - share) * cand[slot, rel, :, span].astype(f32))
        ball[core, chip, :, span] = jnp.concatenate(parts, axis=0).astype(bf16)

    def place(b, dy):
        return ball.at[core, lax.rem(zl + b, Z_LO) * Y + lax.rem(y + dy, Y)]

    pending = []
    across = remote(place(0, 0), place(0, 0), send_z, recv_z, device(dl=1))
    across.start()
    pending.append(across)

    def ring(way, b, hop):
        step = 1 if way == 0 else Y - 1
        block = place(b, (Y - step) * (hop - 1) % Y)
        return remote(block, block, send_y.at[way, b, hop - 1], recv_y.at[way, b, hop - 1], device(dy=step))

    def to_sibling(b, dy):
        block = place(b, dy)
        return remote(block, block, send_s.at[b, dy], recv_s.at[b, dy], device(dh=1))

    def start(copy):
        copy.start()
        pending.append(copy)
        return copy

    rings = {}
    siblings = []
    for way in range(2):
        rings[way, 0, 1] = start(ring(way, 0, 1))
    siblings.append(start(to_sibling(0, 0)))
    across.wait_recv()
    for way in range(2):
        rings[way, 1, 1] = start(ring(way, 1, 1))
    siblings.append(start(to_sibling(1, 0)))

    def last_hop(way, b):
        return HOPS if way == b else HOPS - 1

    for hop in range(1, HOPS + 1):
        for b in range(2):
            for way in range(2):
                if hop > last_hop(way, b):
                    continue
                rings[way, b, hop].wait_recv()
                if hop < last_hop(way, b):
                    rings[way, b, hop + 1] = start(ring(way, b, hop + 1))
                siblings.append(start(to_sibling(b, (hop if way else Y - hop) % Y)))
    for copy in siblings:
        copy.wait_recv()

    def flip(t, carry):
        at = pl.ds(pl.multiple_of(t * 128, 128), 128)
        for h in range(2):
            rows = pl.ds(pl.multiple_of(h * HALF + t * 128, 128), 128)
            for b in range(Z_LO):
                block = ball[h, b * Y : (b + 1) * Y, :, at].reshape(Y * K_CHIP, 128)
                blend_t[rows, b * Y * K_CHIP : (b + 1) * Y * K_CHIP] = block.T
        return carry

    lax.fori_loop(0, HALF // 128, flip, 0)
    for copy in loads:
        copy.wait()

    writes, sums = [], []
    for f in range(NF):
        cols = slice(f * FB, (f + 1) * FB)

        def forward(t, carry, cols=cols):
            rows = pl.ds(pl.multiple_of(t * TILE, TILE), TILE)
            product = jnp.dot(blend_t[rows, :], weight[:, cols], preferred_element_type=f32)
            preact = earlier[rows, cols].astype(f32) + product + bias[:, cols]
            normal_cdf = 0.5 * (1.0 + lax.erf(preact * 0.7071067811865476))
            density = jnp.exp(-0.5 * preact * preact) * 0.3989422804014327
            hidden[rows, cols] = (preact * normal_cdf).astype(bf16)
            grad[rows, :] = (cot[rows, cols].astype(f32) * (normal_cdf + preact * density)).astype(bf16)
            return carry

        lax.fori_loop(0, TOK // TILE, forward, 0)
        write = pltpu.make_async_copy(hidden.at[:, cols], hidden_out.at[:, cols], local_out.at[f])
        write.start()
        writes.append(write)
        out = []
        for d in (2, 1, 3, 0):
            to_x = lax.rem(x + d, X)
            chips = pl.ds(to_x * (CHIPS // X), CHIPS // X)
            total = jnp.dot(
                ball[0, chips].reshape(X_ROWS, HALF), grad[:HALF, :], preferred_element_type=f32
            ) + jnp.dot(ball[1, chips].reshape(X_ROWS, HALF), grad[HALF:, :], preferred_element_type=f32)
            term[f, d] = total.astype(bf16)
            if d:
                out.append(start(remote(term.at[f, d], rx.at[f, d - 1], send_rx.at[f, d - 1], recv_rx.at[f, d - 1], device(dx=d))))
        sums.append(out)

    ends = []
    for f in range(NF):
        for copy in sums[f]:
            copy.wait_recv()
        for q in range(Z_HI):
            rows = slice(q * OUT_ROWS, (q + 1) * OUT_ROWS)
            total = term[f, 0, rows, :].astype(f32)
            for d in range(1, X):
                total = total + rx[f, d - 1, rows, :].astype(f32)
            zs[f, q] = total.astype(bf16)
        out = []
        for d in (2, 1, 3):
            out.append(
                start(remote(zs.at[f, lax.rem(zh + d, Z_HI)], rz.at[f, d - 1], send_rz.at[f, d - 1], recv_rz.at[f, d - 1], device(dz=d)))
            )
        ends.append(out)
    for f in range(NF):
        for copy in ends[f]:
            copy.wait_recv()
        total = zs[f, zh].astype(f32)
        for d in range(1, Z_HI):
            total = total + rz[f, d - 1].astype(f32)
        grad_out[:, f * FB : (f + 1) * FB] = total

    for copy in first + second + pending:
        copy.wait_send()
    for copy in writes:
        copy.wait()


def local(activations, partner, mix_weight, weight, bias, earlier, cotangent):
    bf16, dma = jnp.bfloat16, pltpu.SemaphoreType.DMA
    hbm, vmem, smem = (pl.BlockSpec(memory_space=s) for s in (pl.ANY, pltpu.VMEM, pltpu.SMEM))
    return pl.pallas_call(
        kernel,
        out_shape=(
            jax.ShapeDtypeStruct((TOK, FF_DEV), bf16),
            jax.ShapeDtypeStruct((OUT_ROWS, FF_DEV), jnp.float32),
        ),
        in_specs=[smem, smem, hbm, hbm, vmem, hbm, hbm],
        out_specs=(hbm, vmem),
        scratch_shapes=[
            pltpu.VMEM((X, K_DEV, TOK), bf16),
            pltpu.VMEM((X * 4, K_DEV, PATCHES), bf16),
            pltpu.VMEM((2, K_DEV, HALF), bf16),
            pltpu.VMEM((Z_HI, 2, K_DEV, HALF), bf16),
            pltpu.VMEM((Z_HI, 2, K_DEV, HALF), bf16),
            pltpu.VMEM((2, CHIPS, K_CHIP, HALF), bf16),
            pltpu.VMEM((TOK, K_ALL), bf16),
            pltpu.VMEM((K_ALL, FF_DEV), bf16),
            pltpu.VMEM((TOK, FF_DEV), bf16),
            pltpu.VMEM((TOK, FF_DEV), bf16),
            pltpu.VMEM((TOK, FF_DEV), bf16),
            pltpu.VMEM((TOK, FB), bf16),
            pltpu.VMEM((NF, X, X_ROWS, FB), bf16),
            pltpu.VMEM((NF, X - 1, X_ROWS, FB), bf16),
            pltpu.VMEM((NF, Z_HI, OUT_ROWS, FB), bf16),
            pltpu.VMEM((NF, Z_HI - 1, OUT_ROWS, FB), bf16),
            dma((X,)), dma((X,)),
            dma((Z_HI, 2)), dma((Z_HI, 2)),
            dma, dma,
            dma((2, 2, HOPS)), dma((2, 2, HOPS)),
            dma((2, Y)), dma((2, Y)),
            dma((NF, X - 1)), dma((NF, X - 1)),
            dma((NF, Z_HI - 1)), dma((NF, Z_HI - 1)),
            dma((2,)), dma((3,)), dma((NF,)),
        ],
        compiler_params=pltpu.CompilerParams(
            collective_id=0, has_side_effects=True, vmem_limit_bytes=56 * 2**20
        ),
    )(partner, mix_weight, activations.T, weight, bias.reshape(1, FF_DEV), earlier, cotangent)


def solution(mesh):
    return jax.shard_map(
        local,
        mesh=mesh,
        in_specs=(P("row", "col"), P(), P(), P(None, "col"), P("col"), P("row", "col"), P("row", "col")),
        out_specs=(P("row", "col"), P("row", "col")),
        check_vma=False,
    )
```

time: 236 us -> 74.6 us (0.32)
  waiting for transfers between devices: 160 us -> 0 us
  Pallas kernels: 0 us -> 69.1 us
  blocking collectives: 48.1 us -> 0 us
  between operations: 14.1 us -> 0.65 us
  matrix products: 8.38 us -> 0 us
  local copies, waits for them, and re-layouts: 0.72 us -> 4.62 us
  other arithmetic: 3.03 us -> 0 us
    reduce_scatter x1 -> x0, waiting for transfers between devices: 90.5 us -> none  [local(): lax.psum_scatter(lax.dot_general(gathered, grad_pre, (((0,), (0,)), ((),...]
    all_gather x1 -> x0, waiting for transfers between devices: 69.7 us -> none  [local(): gathered = lax.all_gather(blended, 'col', axis=1, tiled=True)]
    pallas_call x0 -> x1, Pallas kernels: none -> 69.1 us  [local(): pl.pallas_call(kernel, out_shape=(jax.ShapeDtypeStruct((TOK, FF_DEV), bf1...]
    all_gather x1 -> x0, blocking collectives: 48.1 us -> none  [local(): every_image = lax.all_gather(activations, 'row', axis=0, tiled=True)]
    dot_general x2 -> x0, matrix products: 8.38 us -> none  [the longest x1 5.21 us: local(): product = jnp.dot(gathered, weight, preferred_element_type=jnp.float32)]
    unnamed x15 -> x4, local copies, waits for them, and re-layouts: 0.11 us -> 3.35 us
  transfers between devices with their start and end apart: 2 -> 0, of which waited for: 2 -> 0; matrix products, arithmetic and copies ran while one was open for 0% -> 0% of each run, Pallas kernels for 0% -> 0%
where the time goes in v1:
time: 74.6 us; the launch traced here: 74.4 us
  Pallas kernels  69.1 us (93%)
  local copies, waits for them, and re-layouts  4.62 us (6%)
    pallas_call x1, Pallas kernels, local(): pl.pallas_call(kernel, out_shape=(jax.ShapeDtypeStruct((TOK, FF_DEV), bf1...  69.1 us
    unnamed x4, local copies, waits for them, and re-layouts  3.35 us

profile of v1, /device:TPU:1, one launch (start us, length us, event | category | flops | bytes accessed | tf_op | source)
XLA Modules:
  0.0 74.4 jit_solution(6321473247229965433)
XLA Ops:
  0.6 1.3 %reshape.7.bias = f32[1,768]{1,0:T(1,128)} reshape(f32[768]{0:T(1024)} %param.11) | data formatting | bytes 6144 | tf_op jit(solution)/shard_map/reshape | solution.py:277
  1.9 69.1 %shard_map.86 = (bf16[1024,768]{1,0:T(8,128)(2,1)}, f32[48,768]{1,0:T(8,128)}) custom-call(s32[64]{0:T(128)} %partner.1, s32[64]{0:T(128)} %mix.1, bf16[24,1024]{1,0:T(8,128)(2,1)} %bitcast.1, bf16[768,768]{1,0:T(8,128)(2,1)} %weight_in.1, f32[1,768]{1,0:T(1,128)} %reshape.7.bias, bf16[1024,768]{1,0:T(8,128)(2,1)} %earlier_in.1, bf16[1024,768]{1,0:T(8,128)(2,1)} %cot_in.1), custom_call_target="tpu_custom_call" | custom-call | tf_op jit(solution)/shard_map/pallas_call | solution.py:240
  71.0 0.0 copy-start
  71.0 2.7 %copy.11 = bf16[1024,768]{1,0:T(8,128)(2,1)} copy(bf16[1024,768]{1,0:T(8,128)(2,1)} %get-tuple-element.4) | data formatting | bytes 3145728
  73.7 0.0 copy-done
  73.7 0.7 copy.12
Async XLA Ops:
  71.0 2.7 %copy-start = (f32[48,768]{1,0:T(8,128)S(1)}, f32[48,768]{1,0:T(8,128)}, u32[]{:S(2)}) copy-start(f32[48,768]{1,0:T(8,128)} %get-tuple-element.5) | copy-start | bytes 442372

commit v2 on v1

v2 whole, which is shorter than its diff:
```python
import jax
import jax.numpy as jnp
from jax import lax
from jax.experimental import pallas as pl
from jax.experimental.pallas import tpu as pltpu
from jax.sharding import PartitionSpec as P

X, Z_HI, Z_LO, Y = 4, 4, 2, 8
CHIPS = Z_LO * Y
PATCHES = 256
HALF = 512
TOK = 1024
K_DEV, K_CHIP, K_ALL = 24, 48, 768
FF_DEV, FB = 768, 256
NF = FF_DEV // FB
X_ROWS, OUT_ROWS = K_ALL // X, K_ALL // (X * Z_HI)
TILE = 256


def kernel(
    partner, mix, act, weight_in, bias_in, earlier_in, cot_in,
    hidden, grad_out,
    ax, images, own, sel, cand, ball, blend_t, weight, bias, earlier, cot, grad, zterm, zin, term, rx, zs, rz,
    send_a, recv_a, send_p, recv_p, send_y, recv_y, send_l, recv_l, send_d, send_s, recv_s,
    send_rx, recv_rx, send_rz, recv_rz, local_a, local_in,
):
    row, col = lax.axis_index("row"), lax.axis_index("col")
    x, zh = lax.div(row, Z_HI), lax.rem(row, Z_HI)
    chip, core = lax.div(col, 2), lax.rem(col, 2)
    zl, y = lax.div(chip, Y), lax.rem(chip, Y)
    other_core = 1 - core
    f32, bf16 = jnp.float32, jnp.bfloat16

    def device(dx=0, dz=0, dl=0, dy=0, dh=0):
        r = lax.rem(x + dx, X) * Z_HI + lax.rem(zh + dz, Z_HI)
        c = (lax.rem(zl + dl, Z_LO) * Y + lax.rem(y + dy, Y)) * 2 + lax.rem(core + dh, 2)
        return {"row": r, "col": c}

    def remote(src, dst, send, recv, to):
        return pltpu.make_async_remote_copy(
            src_ref=src, dst_ref=dst, send_sem=send, recv_sem=recv,
            device_id=to, device_id_type=pl.DeviceIdType.MESH,
        )

    loads = [
        pltpu.make_async_copy(weight_in, weight, local_in.at[0]),
        pltpu.make_async_copy(bias_in, bias, local_in.at[3]),
        pltpu.make_async_copy(earlier_in, earlier, local_in.at[1]),
        pltpu.make_async_copy(cot_in, cot, local_in.at[2]),
    ]
    mine = [
        pltpu.make_async_copy(act, ax.at[x], local_a.at[0]),
        pltpu.make_async_copy(act.at[:, pl.ds(pl.multiple_of(core * HALF, HALF), HALF)], own.at[0], local_a.at[1]),
    ]
    for copy in mine:
        copy.start()

    barrier = pltpu.get_barrier_semaphore()
    peers = [device(dx=d) for d in range(1, X)]
    peers += [device(dz=d, dh=h) for d in range(Z_HI) for h in range(2) if d or h]
    peers += [device(dl=1)] + [device(dl=l, dy=d) for l in range(Z_LO) for d in (1, 2, Y - 2, Y - 1)]
    for peer in peers:
        pl.semaphore_signal(barrier, inc=1, device_id=peer, device_id_type=pl.DeviceIdType.MESH)
    pl.semaphore_wait(barrier, len(peers))

    first = [remote(act, ax.at[x], send_a.at[d], recv_a.at[d], device(dx=d)) for d in (2, 1, 3)]
    first.append(
        remote(
            act.at[:, pl.ds(pl.multiple_of(other_core * HALF, HALF), HALF)],
            own.at[1], send_a.at[0], recv_a.at[0], device(dh=1),
        )
    )
    for copy in first:
        copy.start()
    for copy in loads:
        copy.start()
    mine[0].wait()
    for copy in first[:3]:
        copy.wait_recv()
    for i in range(X):
        for j in range(4):
            images[i * 4 + j] = ax[i, :, j * PATCHES : (j + 1) * PATCHES]

    second = []
    for d, h in ((2, 0), (2, 1), (1, 0), (1, 1), (3, 0), (3, 1), (0, 1), (0, 0)):
        to_row = x * Z_HI + lax.rem(zh + d, Z_HI)
        to_core = lax.rem(core + h, 2)
        for i in range(2):
            image = partner[to_row * 4 + to_core * 2 + i]
            value = images[lax.div(image, 16) * 4 + lax.rem(image, 4)]
            span = slice(i * PATCHES, (i + 1) * PATCHES)
            if d or h:
                sel[d, h, :, span] = value
            else:
                cand[0, 0, :, span] = value
        if d or h:
            copy = remote(sel.at[d, h], cand.at[d, h], send_p.at[d, h], recv_p.at[d, h], device(dz=d, dh=h))
            copy.start()
            second.append(copy)
    mine[1].wait()
    first[3].wait_recv()
    for copy in second:
        copy.wait_recv()

    for i in range(2):
        image = row * 4 + core * 2 + i
        source = lax.rem(lax.div(partner[image], 4), Z_HI)
        slot = lax.rem(zh - source + Z_HI, Z_HI)
        share = mix[image].astype(f32) / 256.0
        span = slice(i * PATCHES, (i + 1) * PATCHES)
        parts = []
        for k in range(2):
            rel = lax.rem(core + k, 2)
            parts.append(share * own[rel, :, span].astype(f32) + (1.0 - share) * cand[slot, rel, :, span].astype(f32))
        ball[core, chip, :, span] = jnp.concatenate(parts, axis=0).astype(bf16)

    pending = []

    def start(copy):
        copy.start()
        pending.append(copy)
        return copy

    def place(plane, dy):
        return ball.at[core, lax.rem(zl + plane, Z_LO) * Y + lax.rem(y + dy, Y)]

    def along_y(off, step, at=None):
        block, at = place(0, off), (off - step) % Y if at is None else at
        start(remote(block, block, send_y.at[at], recv_y.at[at], device(dy=step)))

    def aslant(off, step, at):
        block = place(0, off)
        start(remote(block, block, send_d.at[at], recv_l.at[at], device(dl=1, dy=step)))

    def to_sibling(plane, off):
        block = place(plane, off)
        start(remote(block, block, send_s.at[plane, off], recv_s.at[plane, off], device(dh=1)))

    def spread(off):
        block = place(0, off)
        start(remote(block, block, send_l.at[off], recv_l.at[off], device(dl=1)))
        to_sibling(0, off)

    def arrival(recv, plane, off):
        block = place(plane, off)
        pltpu.make_async_copy(block, block, recv.at[off]).wait()

    along_y(0, 2)
    along_y(0, 6)
    along_y(0, 1)
    along_y(0, 7)
    spread(0)
    for off in (7, 1):
        arrival(recv_y, 0, off)
        spread(off)
    for off in (6, 2):
        arrival(recv_y, 0, off)
    half_way, onward = 6 - 4 * core, 2 + 4 * core
    along_y(half_way, onward, 4)
    aslant(half_way, onward, 4)
    for off, step in ((6, 1), (2, 7)):
        along_y(off, step)
        aslant(off, step, (off - step) % Y)
    for off in (6, 2):
        spread(off)
    for off in (0, 7, 1, 6, 2):
        arrival(recv_l, 1, off)
        to_sibling(1, off)
    for off in (5, 3, 4):
        arrival(recv_y, 0, off)
        to_sibling(0, off)
    for off in (5, 3, 4):
        arrival(recv_l, 1, off)
        to_sibling(1, off)
    for plane in range(Z_LO):
        for off in range(Y):
            block = ball.at[other_core, lax.rem(zl + plane, Z_LO) * Y + lax.rem(y + off, Y)]
            pltpu.make_async_copy(block, block, recv_s.at[plane, off]).wait()

    def flip(t, carry):
        at = pl.ds(pl.multiple_of(t * 128, 128), 128)
        for h in range(2):
            rows = pl.ds(pl.multiple_of(h * HALF + t * 128, 128), 128)
            for b in range(Z_LO):
                block = ball[h, b * Y : (b + 1) * Y, :, at].reshape(Y * K_CHIP, 128)
                blend_t[rows, b * Y * K_CHIP : (b + 1) * Y * K_CHIP] = block.T
        return carry

    lax.fori_loop(0, HALF // 128, flip, 0)
    for copy in loads:
        copy.wait()

    def forward(f):
        cols = slice(f * FB, (f + 1) * FB)
        for t in range(TOK // TILE):
            rows = slice(t * TILE, (t + 1) * TILE)
            product = jnp.dot(blend_t[rows, :], weight[:, cols], preferred_element_type=f32)
            preact = earlier[rows, cols].astype(f32) + product + bias[cols]
            normal_cdf = 0.5 * (1.0 + lax.erf(preact * 0.7071067811865476))
            density = jnp.exp(-0.5 * preact * preact) * 0.3989422804014327
            hidden[rows, cols] = (preact * normal_cdf).astype(bf16)
            grad[rows, :] = (cot[rows, cols].astype(f32) * (normal_cdf + preact * density)).astype(bf16)

    def terms(to_x):
        chips = pl.ds(to_x * (CHIPS // X), CHIPS // X)
        return jnp.dot(
            ball[0, chips].reshape(X_ROWS, HALF), grad[:HALF, :], preferred_element_type=f32
        ) + jnp.dot(ball[1, chips].reshape(X_ROWS, HALF), grad[HALF:, :], preferred_element_type=f32)

    def over_x(f, d, src, dst):
        return start(remote(src, dst, send_rx.at[f, d - 1], recv_rx.at[f, d - 1], device(dx=d)))

    def over_z(f, d, src, dst):
        return start(remote(src, dst, send_rz.at[f, d - 1], recv_rz.at[f, d - 1], device(dz=d)))

    forward(0)
    for to_x in range(X):
        total = terms(to_x).astype(bf16)
        for q in range(Z_HI):
            zterm[q, to_x] = total[q * OUT_ROWS : (q + 1) * OUT_ROWS, :]
    begun = {0: [over_z(0, d, zterm.at[lax.rem(zh + d, Z_HI)], zin.at[d - 1]) for d in (2, 1, 3)]}
    for f in range(1, NF):
        forward(f)
        begun[f] = []
        for d in (2, 1, 3, 0):
            term[f - 1, d] = terms(lax.rem(x + d, X)).astype(bf16)
            if d:
                begun[f].append(over_x(f, d, term.at[f - 1, d], rx.at[f - 1, d - 1]))

    ends = {}
    for f in range(NF):
        for copy in begun[f]:
            copy.wait_recv()
        if f == 0:
            for to_x in range(X):
                total = zterm[zh, to_x].astype(f32)
                for d in range(1, Z_HI):
                    total = total + zin[d - 1, to_x].astype(f32)
                zs[0, to_x] = total.astype(bf16)
            ends[f] = [over_x(0, d, zs.at[0, lax.rem(x + d, X)], rz.at[0, d - 1]) for d in (2, 1, 3)]
        else:
            for q in range(Z_HI):
                rows = slice(q * OUT_ROWS, (q + 1) * OUT_ROWS)
                total = term[f - 1, 0, rows, :].astype(f32)
                for d in range(1, X):
                    total = total + rx[f - 1, d - 1, rows, :].astype(f32)
                zs[f, q] = total.astype(bf16)
            ends[f] = [over_z(f, d, zs.at[f, lax.rem(zh + d, Z_HI)], rz.at[f, d - 1]) for d in (2, 1, 3)]
    for f in range(NF):
        for copy in ends[f]:
            copy.wait_recv()
        total = zs[f, zh if f else x].astype(f32)
        for d in range(1, Z_HI):
            total = total + rz[f, d - 1].astype(f32)
        grad_out[:, f * FB : (f + 1) * FB] = total

    for copy in first + second + pending:
        copy.wait_send()


def local(activations, partner, mix_weight, weight, bias, earlier, cotangent):
    bf16, dma = jnp.bfloat16, pltpu.SemaphoreType.DMA
    hbm, vmem, smem = (pl.BlockSpec(memory_space=s) for s in (pl.ANY, pltpu.VMEM, pltpu.SMEM))
    return pl.pallas_call(
        kernel,
        out_shape=(
            pltpu.VMEM((TOK, FF_DEV), bf16),
            pltpu.VMEM((OUT_ROWS, FF_DEV), jnp.float32),
        ),
        in_specs=[smem, smem, hbm, hbm, hbm, hbm, hbm],
        out_specs=(vmem, vmem),
        scratch_shapes=[
            pltpu.VMEM((X, K_DEV, TOK), bf16),
            pltpu.VMEM((X * 4, K_DEV, PATCHES), bf16),
            pltpu.VMEM((2, K_DEV, HALF), bf16),
            pltpu.VMEM((Z_HI, 2, K_DEV, HALF), bf16),
            pltpu.VMEM((Z_HI, 2, K_DEV, HALF), bf16),
            pltpu.VMEM((2, CHIPS, K_CHIP, HALF), bf16),
            pltpu.VMEM((TOK, K_ALL), bf16),
            pltpu.VMEM((K_ALL, FF_DEV), bf16),
            pltpu.VMEM((FF_DEV,), jnp.float32),
            pltpu.VMEM((TOK, FF_DEV), bf16),
            pltpu.VMEM((TOK, FF_DEV), bf16),
            pltpu.VMEM((TOK, FB), bf16),
            pltpu.VMEM((Z_HI, X, OUT_ROWS, FB), bf16),
            pltpu.VMEM((Z_HI - 1, X, OUT_ROWS, FB), bf16),
            pltpu.VMEM((NF - 1, X, X_ROWS, FB), bf16),
            pltpu.VMEM((NF - 1, X - 1, X_ROWS, FB), bf16),
            pltpu.VMEM((NF, Z_HI, OUT_ROWS, FB), bf16),
            pltpu.VMEM((NF, Z_HI - 1, OUT_ROWS, FB), bf16),
            dma((X,)), dma((X,)),
            dma((Z_HI, 2)), dma((Z_HI, 2)),
            dma((Y,)), dma((Y,)), dma((Y,)), dma((Y,)), dma((Y,)),
            dma((2, Y)), dma((2, Y)),
            dma((NF, X - 1)), dma((NF, X - 1)),
            dma((NF, Z_HI - 1)), dma((NF, Z_HI - 1)),
            dma((2,)), dma((4,)),
        ],
        compiler_params=pltpu.CompilerParams(
            collective_id=0, has_side_effects=True, vmem_limit_bytes=56 * 2**20
        ),
    )(partner, mix_weight, activations.T, weight, bias, earlier, cotangent)


def solution(mesh):
    return jax.shard_map(
        local,
        mesh=mesh,
        in_specs=(P("row", "col"), P(), P(), P(None, "col"), P("col"), P("row", "col"), P("row", "col")),
        out_specs=(P("row", "col"), P("row", "col")),
        check_vma=False,
    )
```

time: 74.6 us -> 66.3 us (0.89)
  Pallas kernels: 69.1 us -> 63.7 us
  local copies, waits for them, and re-layouts: 4.62 us -> 1.81 us
    pallas_call x1, Pallas kernels: 69.1 us -> 63.7 us  [local(): pl.pallas_call(kernel, out_shape=(pltpu.VMEM((TOK, FF_DEV), bf16), pltpu....]
    unnamed x4 -> x2, local copies, waits for them, and re-layouts: 3.35 us -> 1.81 us
    reshape x1 -> x0, local copies, waits for them, and re-layouts: 1.27 us -> none  [local(): bias.reshape(1, FF_DEV)]
where the time goes in v2:
time: 66.3 us; the launch traced here: 66.2 us
  Pallas kernels  63.7 us (96%)
  local copies, waits for them, and re-layouts  1.81 us (3%)
    pallas_call x1, Pallas kernels, local(): pl.pallas_call(kernel, out_shape=(pltpu.VMEM((TOK, FF_DEV), bf16), pltpu....  63.7 us
    unnamed x2, local copies, waits for them, and re-layouts  1.81 us

profile of v2, /device:TPU:1, one launch (start us, length us, event | category | flops | bytes accessed | tf_op | source)
XLA Modules:
  0.0 66.2 jit_solution(5815581111693085865)
XLA Ops:
  0.6 63.7 %shard_map.86 = (bf16[1024,768]{1,0:T(8,128)(2,1)S(1)}, f32[48,768]{1,0:T(8,128)S(1)}) custom-call(s32[64]{0:T(128)} %partner.1, s32[64]{0:T(128)} %mix.1, bf16[24,1024]{1,0:T(8,128)(2,1)} %bitcast.1, bf16[768,768]{1,0:T(8,128)(2,1)} %weight_in.1, f32[768]{0:T(1024)} %bias_in.1, bf16[1024,768]{1,0:T(8,128)(2,1)} %earlier_in.1, bf16[1024,768]{1,0:T(8,128)(2,1)} %cot_in.1), custom_call_target="tpu_custom_call" | custom-call | tf_op jit(solution)/shard_map/pallas_call | solution.py:264
  64.4 1.1 %copy.11 = bf16[1024,768]{1,0:T(8,128)(2,1)} copy(bf16[1024,768]{1,0:T(8,128)(2,1)S(1)} %get-tuple-element.2) | data formatting | bytes 3145728
  65.5 0.7 copy.12

commit v3 on v2

v3 whole, which is shorter than its diff:
```python
import jax
import jax.numpy as jnp
from jax import lax
from jax.experimental import pallas as pl
from jax.experimental.pallas import tpu as pltpu
from jax.sharding import PartitionSpec as P

X, Z_HI, Z_LO, Y = 4, 4, 2, 8
CHIPS = Z_LO * Y
PATCHES = 256
HALF = 512
TOK = 1024
K_DEV, K_CHIP, K_ALL = 24, 48, 768
FF_DEV = 768
BLOCKS = ((0, 256), (256, 256), (512, 128), (640, 128))
ORDER = (1, 0, 2, 3)
FB, NF = 256, len(BLOCKS)
X_ROWS, OUT_ROWS = K_ALL // X, K_ALL // (X * Z_HI)
TILE = 256


def kernel(
    partner, mix, act, weight_in, bias_in, earlier_in, cot_in,
    hidden, grad_out,
    ax, images, own, sel, cand_0, cand_1, ball, blend_t, weight, bias, earlier, cot, grad, zterm, zin, term, rx, zs, rz,
    send_a, recv_a, send_p, recv_p, send_y, recv_y, send_d, recv_d, send_l, recv_l, send_s, recv_s,
    send_rx, recv_rx, send_rz, recv_rz, local_a, local_in,
):
    row, col = lax.axis_index("row"), lax.axis_index("col")
    x, zh = lax.div(row, Z_HI), lax.rem(row, Z_HI)
    chip, core = lax.div(col, 2), lax.rem(col, 2)
    zl, y = lax.div(chip, Y), lax.rem(chip, Y)
    other_core = 1 - core
    f32, bf16 = jnp.float32, jnp.bfloat16

    def device(dx=0, dz=0, dl=0, dy=0, dh=0):
        r = lax.rem(x + dx, X) * Z_HI + lax.rem(zh + dz, Z_HI)
        c = (lax.rem(zl + dl, Z_LO) * Y + lax.rem(y + dy, Y)) * 2 + lax.rem(core + dh, 2)
        return {"row": r, "col": c}

    def remote(src, dst, send, recv, to):
        return pltpu.make_async_remote_copy(
            src_ref=src, dst_ref=dst, send_sem=send, recv_sem=recv,
            device_id=to, device_id_type=pl.DeviceIdType.MESH,
        )

    loads = [
        pltpu.make_async_copy(weight_in, weight, local_in.at[0]),
        pltpu.make_async_copy(bias_in, bias, local_in.at[3]),
        pltpu.make_async_copy(earlier_in, earlier, local_in.at[1]),
        pltpu.make_async_copy(cot_in, cot, local_in.at[2]),
    ]
    mine = [
        pltpu.make_async_copy(act, ax.at[x], local_a.at[0]),
        pltpu.make_async_copy(act.at[:, pl.ds(pl.multiple_of(core * HALF, HALF), HALF)], own.at[0], local_a.at[1]),
    ]
    for copy in mine:
        copy.start()

    barrier = pltpu.get_barrier_semaphore()
    peers = [device(dx=d) for d in range(1, X)]
    peers += [device(dz=d, dh=h) for d in range(Z_HI) for h in range(2) if d or h]
    peers += [device(dl=1)] + [device(dl=l, dy=d) for l in range(Z_LO) for d in (1, 2, Y - 2, Y - 1)]
    for peer in peers:
        pl.semaphore_signal(barrier, inc=1, device_id=peer, device_id_type=pl.DeviceIdType.MESH)
    pl.semaphore_wait(barrier, len(peers))

    cand = (cand_0, cand_1)

    first = [remote(act, ax.at[x], send_a.at[d], recv_a.at[d], device(dx=d)) for d in (2, 1, 3)]
    first.append(
        remote(
            act.at[:, pl.ds(pl.multiple_of(other_core * HALF, HALF), HALF)],
            own.at[1], send_a.at[0], recv_a.at[0], device(dh=1),
        )
    )
    for copy in first:
        copy.start()
    for copy in loads:
        copy.start()
    mine[0].wait()
    for copy in first[:3]:
        copy.wait_recv()
    for i in range(X):
        for j in range(4):
            images[i * 4 + j] = ax[i, :, j * PATCHES : (j + 1) * PATCHES]

    second = []
    for i in range(2):
        for d, h in ((2, 0), (2, 1), (1, 0), (1, 1), (3, 0), (3, 1), (0, 1), (0, 0)):
            to_row = x * Z_HI + lax.rem(zh + d, Z_HI)
            image = partner[to_row * 4 + lax.rem(core + h, 2) * 2 + i]
            value = images[lax.div(image, 16) * 4 + lax.rem(image, 4)]
            if d or h:
                sel[i, d, h] = value
                copy = remote(sel.at[i, d, h], cand[i].at[d, h], send_p.at[i, d, h], recv_p.at[i, d, h], device(dz=d, dh=h))
                copy.start()
                second.append(copy)
            else:
                cand[i][0, 0] = value
    mine[1].wait()
    first[3].wait_recv()

    def blend(i):
        for copy in second[7 * i : 7 * i + 7]:
            copy.wait_recv()
        image = row * 4 + core * 2 + i
        source = lax.rem(lax.div(partner[image], 4), Z_HI)
        slot = lax.rem(zh - source + Z_HI, Z_HI)
        share = mix[image].astype(f32) / 256.0
        span = slice(i * PATCHES, (i + 1) * PATCHES)
        parts = []
        for k in range(2):
            rel = lax.rem(core + k, 2)
            parts.append(share * own[rel, :, span].astype(f32) + (1.0 - share) * cand[i][slot, rel].astype(f32))
        ball[core, chip, :, span] = jnp.concatenate(parts, axis=0).astype(bf16)

    pending = []

    def start(copy):
        copy.start()
        pending.append(copy)
        return copy

    def place(plane, dy):
        return ball.at[core, lax.rem(zl + plane, Z_LO) * Y + lax.rem(y + dy, Y)]

    def image_of(off, i):
        return place(0, off).at[:, i * PATCHES : (i + 1) * PATCHES]

    def along_y(i, off, step, at):
        block = image_of(off, i)
        start(remote(block, block, send_y.at[i, at], recv_y.at[i, at], device(dy=step)))

    def aslant(i, off, step, at):
        block = image_of(off, i)
        start(remote(block, block, send_d.at[i, at], recv_d.at[i, at], device(dl=1, dy=step)))

    def to_sibling(plane, off):
        block = place(plane, off)
        start(remote(block, block, send_s.at[plane, off], recv_s.at[plane, off], device(dh=1)))

    def wait_for(block, sem):
        pltpu.make_async_copy(block, block, sem).wait()

    def onward(i):
        for off in (6, 2):
            wait_for(image_of(off, i), recv_y.at[i, off])
        off, step = 6 - 4 * core, 2 + 4 * core
        along_y(i, off, step, 4)
        aslant(i, off, step, 4)
        for off, step, at in ((6, 1, 5), (2, 7, 3)):
            along_y(i, off, step, at)
            aslant(i, off, step, at)

    def across(off):
        block = place(0, off)
        start(remote(block, block, send_l.at[off], recv_l.at[off], device(dl=1)))

    for i in range(2):
        blend(i)
        if i:
            across(0)
        for step in (2, 6, 1, 7):
            along_y(i, 0, step, Y - step)
    to_sibling(0, 0)
    block = place(1, 0)
    wait_for(block, recv_l.at[0])
    for step in (1, 7):
        start(remote(block, block, send_l.at[Y - step], recv_l.at[Y - step], device(dy=step)))
    to_sibling(1, 0)
    onward(0)
    for off in (7, 1):
        for i in range(2):
            wait_for(image_of(off, i), recv_y.at[i, off])
        to_sibling(0, off)
    onward(1)
    for off in (6, 2):
        across(off)
        to_sibling(0, off)
    for off in (7, 1, 6, 2):
        wait_for(place(1, off), recv_l.at[off])
        to_sibling(1, off)
    for off in (5, 3, 4):
        for i in range(2):
            wait_for(image_of(off, i), recv_y.at[i, off])
        to_sibling(0, off)
    for off in (5, 3, 4):
        for i in range(2):
            wait_for(place(1, off).at[:, i * PATCHES : (i + 1) * PATCHES], recv_d.at[i, off])
        to_sibling(1, off)
    for plane in range(Z_LO):
        for off in range(Y):
            block = ball.at[other_core, lax.rem(zl + plane, Z_LO) * Y + lax.rem(y + off, Y)]
            wait_for(block, recv_s.at[plane, off])

    def flip(t, carry):
        at = pl.ds(pl.multiple_of(t * 128, 128), 128)
        for h in range(2):
            rows = pl.ds(pl.multiple_of(h * HALF + t * 128, 128), 128)
            for b in range(Z_LO):
                block = ball[h, b * Y : (b + 1) * Y, :, at].reshape(Y * K_CHIP, 128)
                blend_t[rows, b * Y * K_CHIP : (b + 1) * Y * K_CHIP] = block.T
        return carry

    lax.fori_loop(0, HALF // 128, flip, 0)
    for copy in loads:
        copy.wait()

    def forward(f):
        at, width = BLOCKS[f]
        cols = slice(at, at + width)
        for t in range(TOK // TILE):
            rows = slice(t * TILE, (t + 1) * TILE)
            product = jnp.dot(blend_t[rows, :], weight[:, cols], preferred_element_type=f32)
            preact = earlier[rows, cols].astype(f32) + product + bias[cols]
            normal_cdf = 0.5 * (1.0 + lax.erf(preact * 0.7071067811865476))
            density = jnp.exp(-0.5 * preact * preact) * 0.3989422804014327
            hidden[rows, cols] = (preact * normal_cdf).astype(bf16)
            grad[rows, :width] = (cot[rows, cols].astype(f32) * (normal_cdf + preact * density)).astype(bf16)

    def terms(load, width):
        total = sum(
            jnp.dot(load(h), grad[h * HALF : (h + 1) * HALF, :width], preferred_element_type=f32) for h in range(2)
        )
        return total.astype(bf16)

    def over_x(f, d, src, dst):
        return start(remote(src, dst, send_rx.at[f, d - 1], recv_rx.at[f, d - 1], device(dx=d)))

    def over_z(f, d, src, dst):
        return start(remote(src, dst, send_rz.at[f, d - 1], recv_rz.at[f, d - 1], device(dz=d)))

    begun = {}
    for f, (at, width) in enumerate(BLOCKS):
        forward(f)
        cols = slice(at, at + width)
        begun[f] = []
        for d in (2, 1, 3, 0):
            if f == 0:
                to_z = lax.rem(zh + d, Z_HI)

                def load(h, to_z=to_z):
                    return jnp.concatenate([ball[h, Z_HI * k + to_z] for k in range(X)], axis=0)

                zterm[d] = terms(load, width).reshape(X, OUT_ROWS, width)
                if d:
                    begun[f].append(over_z(f, d, zterm.at[d], zin.at[d - 1]))
            else:
                to_x = lax.rem(x + d, X)

                def load(h, to_x=to_x):
                    return ball[h, pl.ds(to_x * Z_HI, Z_HI)].reshape(X_ROWS, HALF)

                term[d, :, cols] = terms(load, width)
                if d:
                    begun[f].append(over_x(f, d, term.at[d, :, cols], rx.at[d - 1, :, cols]))

    ends = {}
    for f in ORDER:
        at, width = BLOCKS[f]
        cols = slice(at, at + width)
        for copy in begun[f]:
            copy.wait_recv()
        for q in range(X):
            if f == 0:
                total = zterm[0, q].astype(f32)
                for d in range(1, Z_HI):
                    total = total + zin[d - 1, q].astype(f32)
            else:
                rows = slice(q * OUT_ROWS, (q + 1) * OUT_ROWS)
                total = term[0, rows, cols].astype(f32)
                for d in range(1, X):
                    total = total + rx[d - 1, rows, cols].astype(f32)
            zs[q, :, cols] = total.astype(bf16)
        ends[f] = []
        for d in (2, 1, 3):
            to = lax.rem(zh + d, Z_HI) if f else lax.rem(x + d, X)
            ends[f].append((over_z if f else over_x)(f, d, zs.at[to, :, cols], rz.at[d - 1, :, cols]))
    for f in ORDER:
        at, width = BLOCKS[f]
        cols = slice(at, at + width)
        for copy in ends[f]:
            copy.wait_recv()
        total = zs[zh if f else x, :, cols].astype(f32)
        for d in range(1, Z_HI):
            total = total + rz[d - 1, :, cols].astype(f32)
        grad_out[:, cols] = total

    for copy in first + second + pending:
        copy.wait_send()


def write_out(hidden, grad, hidden_out, grad_out, sems):
    copies = [
        pltpu.make_async_copy(hidden, hidden_out, sems.at[0]),
        pltpu.make_async_copy(grad, grad_out, sems.at[1]),
    ]
    for copy in copies:
        copy.start()
    for copy in copies:
        copy.wait()


def local(activations, partner, mix_weight, weight, bias, earlier, cotangent):
    bf16, dma = jnp.bfloat16, pltpu.SemaphoreType.DMA
    hbm, vmem, smem = (pl.BlockSpec(memory_space=s) for s in (pl.ANY, pltpu.VMEM, pltpu.SMEM))
    hidden, grad = pl.pallas_call(
        kernel,
        out_shape=(
            pltpu.VMEM((TOK, FF_DEV), bf16),
            pltpu.VMEM((OUT_ROWS, FF_DEV), jnp.float32),
        ),
        in_specs=[smem, smem, hbm, hbm, hbm, hbm, hbm],
        out_specs=(vmem, vmem),
        scratch_shapes=[
            pltpu.VMEM((X, K_DEV, TOK), bf16),
            pltpu.VMEM((X * 4, K_DEV, PATCHES), bf16),
            pltpu.VMEM((2, K_DEV, HALF), bf16),
            pltpu.VMEM((2, Z_HI, 2, K_DEV, PATCHES), bf16),
            pltpu.VMEM((Z_HI, 2, K_DEV, PATCHES), bf16),
            pltpu.VMEM((Z_HI, 2, K_DEV, PATCHES), bf16),
            pltpu.VMEM((2, CHIPS, K_CHIP, HALF), bf16),
            pltpu.VMEM((TOK, K_ALL), bf16),
            pltpu.VMEM((K_ALL, FF_DEV), bf16),
            pltpu.VMEM((FF_DEV,), jnp.float32),
            pltpu.VMEM((TOK, FF_DEV), bf16),
            pltpu.VMEM((TOK, FF_DEV), bf16),
            pltpu.VMEM((TOK, FB), bf16),
            pltpu.VMEM((Z_HI, X, OUT_ROWS, FB), bf16),
            pltpu.VMEM((Z_HI - 1, X, OUT_ROWS, FB), bf16),
            pltpu.VMEM((X, X_ROWS, FF_DEV), bf16),
            pltpu.VMEM((X - 1, X_ROWS, FF_DEV), bf16),
            pltpu.VMEM((Z_HI, OUT_ROWS, FF_DEV), bf16),
            pltpu.VMEM((Z_HI - 1, OUT_ROWS, FF_DEV), bf16),
            dma((X,)), dma((X,)),
            dma((2, Z_HI, 2)), dma((2, Z_HI, 2)),
            dma((2, Y)), dma((2, Y)), dma((2, Y)), dma((2, Y)), dma((Y,)), dma((Y,)),
            dma((2, Y)), dma((2, Y)),
            dma((NF, X - 1)), dma((NF, X - 1)),
            dma((NF, Z_HI - 1)), dma((NF, Z_HI - 1)),
            dma((2,)), dma((4,)),
        ],
        compiler_params=pltpu.CompilerParams(
            collective_id=0, has_side_effects=True, vmem_limit_bytes=56 * 2**20
        ),
    )(partner, mix_weight, activations.T, weight, bias, earlier, cotangent)
    hidden, grad = (pltpu.with_memory_space_constraint(a, pltpu.VMEM) for a in (hidden, grad))
    return pl.pallas_call(
        write_out,
        out_shape=(
            jax.ShapeDtypeStruct((TOK, FF_DEV), bf16),
            jax.ShapeDtypeStruct((OUT_ROWS, FF_DEV), jnp.float32),
        ),
        in_specs=[hbm, hbm],
        out_specs=(hbm, hbm),
        scratch_shapes=[dma((2,))],
    )(hidden, grad)


def solution(mesh):
    return jax.shard_map(
        local,
        mesh=mesh,
        in_specs=(P("row", "col"), P(), P(), P(None, "col"), P("col"), P("row", "col"), P("row", "col")),
        out_specs=(P("row", "col"), P("row", "col")),
        check_vma=False,
    )
```

time: 66.3 us -> 62.4 us (0.941)
  Pallas kernels: 63.7 us -> 61.6 us
  local copies, waits for them, and re-layouts: 1.81 us -> 0 us
    pallas_call x1, Pallas kernels: 63.7 us -> 60.4 us  [local(): pl.pallas_call(kernel, out_shape=(pltpu.VMEM((TOK, FF_DEV), bf16), pltpu....]
    unnamed x2 -> x0, local copies, waits for them, and re-layouts: 1.81 us -> none
    pallas_call x0 -> x1, Pallas kernels: none -> 1.2 us  [local(): pl.pallas_call(write_out, out_shape=(jax.ShapeDtypeStruct((TOK, FF_DEV),...]
where the time goes in v3:
time: 62.4 us; the launch traced here: 62.2 us
  Pallas kernels  61.6 us (99%)
  between operations  0.64 us (1%)
    pallas_call x1, Pallas kernels, local(): pl.pallas_call(kernel, out_shape=(pltpu.VMEM((TOK, FF_DEV), bf16), pltpu....  60.4 us

profile of v3, /device:TPU:1, one launch (start us, length us, event | category | flops | bytes accessed | tf_op | source)
XLA Modules:
  0.0 62.2 jit_solution(13708486738308760923)
XLA Ops:
  0.6 60.4 %shard_map.86 = (bf16[1024,768]{1,0:T(8,128)(2,1)S(1)}, f32[48,768]{1,0:T(8,128)S(1)}) custom-call(s32[64]{0:T(128)} %partner.1, s32[64]{0:T(128)} %mix.1, bf16[24,1024]{1,0:T(8,128)(2,1)} %bitcast.1, bf16[768,768]{1,0:T(8,128)(2,1)} %weight_in.1, f32[768]{0:T(1024)} %bias_in.1, bf16[1024,768]{1,0:T(8,128)(2,1)} %earlier_in.1, bf16[1024,768]{1,0:T(8,128)(2,1)} %cot_in.1), custom_call_target="tpu_custom_call" | custom-call | tf_op jit(solution)/shard_map/pallas_call | solution.py:308
  61.0 1.2 %shard_map.87 = (bf16[1024,768]{1,0:T(8,128)(2,1)}, f32[48,768]{1,0:T(8,128)}) custom-call(bf16[1024,768]{1,0:T(8,128)(2,1)S(1)} %get-tuple-element.4.hidden, f32[48,768]{1,0:T(8,128)S(1)} %get-tuple-element.5.grad), custom_call_target="tpu_custom_call" | custom-call | tf_op jit(solution)/shard_map/pallas_call | solution.py:349

commit v4 on v3

--- a/solution.py
+++ b/solution.py
@@ -14,6 +14,7 @@
 FF_DEV = 768
 BLOCKS = ((0, 256), (256, 256), (512, 128), (640, 128))
 ORDER = (1, 0, 2, 3)
+GROUPS = ((0, 1), (2,), (3,))
 FB, NF = 256, len(BLOCKS)
 X_ROWS, OUT_ROWS = K_ALL // X, K_ALL // (X * Z_HI)
 TILE = 256
@@ -189,39 +190,40 @@
         for i in range(2):
             wait_for(place(1, off).at[:, i * PATCHES : (i + 1) * PATCHES], recv_d.at[i, off])
         to_sibling(1, off)
-    for plane in range(Z_LO):
-        for off in range(Y):
-            block = ball.at[other_core, lax.rem(zl + plane, Z_LO) * Y + lax.rem(y + off, Y)]
-            wait_for(block, recv_s.at[plane, off])
-
-    def flip(t, carry):
-        at = pl.ds(pl.multiple_of(t * 128, 128), 128)
-        for h in range(2):
+    def flip(h):
+        for t in range(HALF // 128):
+            at = slice(t * 128, (t + 1) * 128)
             rows = pl.ds(pl.multiple_of(h * HALF + t * 128, 128), 128)
             for b in range(Z_LO):
                 block = ball[h, b * Y : (b + 1) * Y, :, at].reshape(Y * K_CHIP, 128)
                 blend_t[rows, b * Y * K_CHIP : (b + 1) * Y * K_CHIP] = block.T
-        return carry
-
-    lax.fori_loop(0, HALF // 128, flip, 0)
-    for copy in loads:
-        copy.wait()
-
-    def forward(f):
+
+    def forward(f, h):
         at, width = BLOCKS[f]
         cols = slice(at, at + width)
-        for t in range(TOK // TILE):
-            rows = slice(t * TILE, (t + 1) * TILE)
+        for t in range(HALF // TILE):
+            rows = pl.ds(pl.multiple_of(h * HALF + t * TILE, TILE), TILE)
             product = jnp.dot(blend_t[rows, :], weight[:, cols], preferred_element_type=f32)
             preact = earlier[rows, cols].astype(f32) + product + bias[cols]
             normal_cdf = 0.5 * (1.0 + lax.erf(preact * 0.7071067811865476))
             density = jnp.exp(-0.5 * preact * preact) * 0.3989422804014327
             hidden[rows, cols] = (preact * normal_cdf).astype(bf16)
-            grad[rows, :width] = (cot[rows, cols].astype(f32) * (normal_cdf + preact * density)).astype(bf16)
-
-    def terms(load, width):
+            grad[rows, cols] = (cot[rows, cols].astype(f32) * (normal_cdf + preact * density)).astype(bf16)
+
+    for copy in loads:
+        copy.wait()
+    flip(core)
+    for f in range(NF):
+        forward(f, core)
+    for plane in range(Z_LO):
+        for off in range(Y):
+            block = ball.at[other_core, lax.rem(zl + plane, Z_LO) * Y + lax.rem(y + off, Y)]
+            wait_for(block, recv_s.at[plane, off])
+    flip(other_core)
+
+    def terms(load, cols):
         total = sum(
-            jnp.dot(load(h), grad[h * HALF : (h + 1) * HALF, :width], preferred_element_type=f32) for h in range(2)
+            jnp.dot(load(h), grad[h * HALF : (h + 1) * HALF, cols], preferred_element_type=f32) for h in range(2)
         )
         return total.astype(bf16)
 
@@ -231,30 +233,29 @@
     def over_z(f, d, src, dst):
         return start(remote(src, dst, send_rz.at[f, d - 1], recv_rz.at[f, d - 1], device(dz=d)))
 
-    begun = {}
-    for f, (at, width) in enumerate(BLOCKS):
-        forward(f)
+    begun = {f: [] for f in range(NF)}
+
+    def first_sum(f, d):
+        at, width = BLOCKS[f]
         cols = slice(at, at + width)
-        begun[f] = []
+        if f == 0:
+            to_z = lax.rem(zh + d, Z_HI)
+            total = terms(lambda h: jnp.concatenate([ball[h, Z_HI * k + to_z] for k in range(X)], axis=0), cols)
+            zterm[d] = total.reshape(X, OUT_ROWS, width)
+            if d:
+                begun[f].append(over_z(f, d, zterm.at[d], zin.at[d - 1]))
+        else:
+            to_x = lax.rem(x + d, X)
+            term[d, :, cols] = terms(lambda h: ball[h, pl.ds(to_x * Z_HI, Z_HI)].reshape(X_ROWS, HALF), cols)
+            if d:
+                begun[f].append(over_x(f, d, term.at[d, :, cols], rx.at[d - 1, :, cols]))
+
+    for group in GROUPS:
+        for f in group:
+            forward(f, other_core)
         for d in (2, 1, 3, 0):
-            if f == 0:
-                to_z = lax.rem(zh + d, Z_HI)
-
-                def load(h, to_z=to_z):
-                    return jnp.concatenate([ball[h, Z_HI * k + to_z] for k in range(X)], axis=0)
-
-                zterm[d] = terms(load, width).reshape(X, OUT_ROWS, width)
-                if d:
-                    begun[f].append(over_z(f, d, zterm.at[d], zin.at[d - 1]))
-            else:
-                to_x = lax.rem(x + d, X)
-
-                def load(h, to_x=to_x):
-                    return ball[h, pl.ds(to_x * Z_HI, Z_HI)].reshape(X_ROWS, HALF)
-
-                term[d, :, cols] = terms(load, width)
-                if d:
-                    begun[f].append(over_x(f, d, term.at[d, :, cols], rx.at[d - 1, :, cols]))
+            for f in group:
+                first_sum(f, d)
 
     ends = {}
     for f in ORDER:
@@ -326,7 +327,7 @@
             pltpu.VMEM((FF_DEV,), jnp.float32),
             pltpu.VMEM((TOK, FF_DEV), bf16),
             pltpu.VMEM((TOK, FF_DEV), bf16),
-            pltpu.VMEM((TOK, FB), bf16),
+            pltpu.VMEM((TOK, FF_DEV), bf16),
             pltpu.VMEM((Z_HI, X, OUT_ROWS, FB), bf16),
             pltpu.VMEM((Z_HI - 1, X, OUT_ROWS, FB), bf16),
             pltpu.VMEM((X, X_ROWS, FF_DEV), bf16),

time: 62.4 us -> 61.8 us (level)
  Pallas kernels: 61.6 us -> 60.5 us
    pallas_call x1, Pallas kernels: 60.4 us -> 59.3 us  [local(): pl.pallas_call(kernel, out_shape=(pltpu.VMEM((TOK, FF_DEV), bf16), pltpu....]
where the time goes in v4:
time: 61.8 us; the launch traced here: 61.2 us
  Pallas kernels  60.5 us (98%)
  between operations  0.64 us (1%)
    pallas_call x1, Pallas kernels, local(): pl.pallas_call(kernel, out_shape=(pltpu.VMEM((TOK, FF_DEV), bf16), pltpu....  59.3 us

profile of v4, /device:TPU:1, one launch (start us, length us, event | category | flops | bytes accessed | tf_op | source)
XLA Modules:
  0.0 61.2 jit_solution(5494070745976689232)
XLA Ops:
  0.6 59.3 %shard_map.86 = (bf16[1024,768]{1,0:T(8,128)(2,1)S(1)}, f32[48,768]{1,0:T(8,128)S(1)}) custom-call(s32[64]{0:T(128)} %partner.1, s32[64]{0:T(128)} %mix.1, bf16[24,1024]{1,0:T(8,128)(2,1)} %bitcast.1, bf16[768,768]{1,0:T(8,128)(2,1)} %weight_in.1, f32[768]{0:T(1024)} %bias_in.1, bf16[1024,768]{1,0:T(8,128)(2,1)} %earlier_in.1, bf16[1024,768]{1,0:T(8,128)(2,1)} %cot_in.1), custom_call_target="tpu_custom_call" | custom-call | tf_op jit(solution)/shard_map/pallas_call | solution.py:309
  60.0 1.2 %shard_map.87 = (bf16[1024,768]{1,0:T(8,128)(2,1)}, f32[48,768]{1,0:T(8,128)}) custom-call(bf16[1024,768]{1,0:T(8,128)(2,1)S(1)} %get-tuple-element.4.hidden, f32[48,768]{1,0:T(8,128)S(1)} %get-tuple-element.5.grad), custom_call_target="tpu_custom_call" | custom-call | tf_op jit(solution)/shard_map/pallas_call | solution.py:350

commit v5 on v4

--- a/solution.py
+++ b/solution.py
@@ -13,8 +13,8 @@
 K_DEV, K_CHIP, K_ALL = 24, 48, 768
 FF_DEV = 768
 BLOCKS = ((0, 256), (256, 256), (512, 128), (640, 128))
-ORDER = (1, 0, 2, 3)
-GROUPS = ((0, 1), (2,), (3,))
+ORDER = (1, 2, 3, 0)
+GROUPS = ((0,), (1,), (2,), (3,))
 FB, NF = 256, len(BLOCKS)
 X_ROWS, OUT_ROWS = K_ALL // X, K_ALL // (X * Z_HI)
 TILE = 256

time: 61.8 us -> 60.9 us (0.985)
  no operation moved by 1% of the time
where the time goes in v5:
time: 60.9 us; the launch traced here: 60.8 us
  Pallas kernels  60.2 us (99%)
  between operations  0.64 us (1%)
    pallas_call x1, Pallas kernels, local(): pl.pallas_call(kernel, out_shape=(pltpu.VMEM((TOK, FF_DEV), bf16), pltpu....  59 us

profile of v5, /device:TPU:1, one launch (start us, length us, event | category | flops | bytes accessed | tf_op | source)
XLA Modules:
  0.0 60.8 jit_solution(12143647643227725451)
XLA Ops:
  0.6 59.0 %shard_map.86 = (bf16[1024,768]{1,0:T(8,128)(2,1)S(1)}, f32[48,768]{1,0:T(8,128)S(1)}) custom-call(s32[64]{0:T(128)} %partner.1, s32[64]{0:T(128)} %mix.1, bf16[24,1024]{1,0:T(8,128)(2,1)} %bitcast.1, bf16[768,768]{1,0:T(8,128)(2,1)} %weight_in.1, f32[768]{0:T(1024)} %bias_in.1, bf16[1024,768]{1,0:T(8,128)(2,1)} %earlier_in.1, bf16[1024,768]{1,0:T(8,128)(2,1)} %cot_in.1), custom_call_target="tpu_custom_call" | custom-call | tf_op jit(solution)/shard_map/pallas_call | solution.py:309
  59.6 1.2 %shard_map.87 = (bf16[1024,768]{1,0:T(8,128)(2,1)}, f32[48,768]{1,0:T(8,128)}) custom-call(bf16[1024,768]{1,0:T(8,128)(2,1)S(1)} %get-tuple-element.4.hidden, f32[48,768]{1,0:T(8,128)S(1)} %get-tuple-element.5.grad), custom_call_target="tpu_custom_call" | custom-call | tf_op jit(solution)/shard_map/pallas_call | solution.py:350
